TPU v7x, 32 devices: a whole 2x2x4 slice. The times are simulated.
32 devices in a mesh: groups: 2 (over y), rows: 4 (over z), shard: 4 (over x, core).
Axes of the slice: x: 2, y: 2, z: 4, core: 2. Of those that a mesh axis runs over, the one named last changes fastest.
Arguments:
- images: bfloat16 [8, 8, 128, 512], P(('groups', 'shard'), 'rows'), parts along dimension 0, may hold values from -6 to 6
- cotangent: bfloat16 [8, 8, 128, 512], P(('groups', 'shard'), 'rows'), parts along dimension 0, may hold values from -6 to 6
- weight_in: bfloat16 [2, 512, 512], P(None, 'shard'), may hold values from -0.25 to 0.25
- weight_group: bfloat16 [2, 144, 512], P(None, 'shard'), may hold values from -0.5 to 0.5
- weight_out: bfloat16 [2, 512, 512], P(None, 'shard'), may hold values from -0.25 to 0.25
Outputs:
- decoded: bfloat16 [8, 8, 128, 512], P(('groups', 'shard'), 'rows'), parts along dimension 0
- grad_images: bfloat16 [8, 8, 128, 512], P(('groups', 'shard'), 'rows'), parts along dimension 0
- grad_in: float32 [4, 512, 512], P('groups', 'shard'), parts along dimension 0
- grad_group: float32 [4, 144, 512], P('groups', 'shard'), parts along dimension 0
- grad_out: float32 [4, 512, 512], P('groups', 'shard'), parts along dimension 0
There are 2 independent parts, one for each index of `groups`. A program takes and returns all parts, laid end to end along the dimension named above; an argument that names none is the same for every part. Nothing has to cross between parts.
All inputs are finite; a program needn't handle non-finite values.
Results may differ from a plain program's by a relative error of at most 0.02.
Values may be sent and summed in bfloat16 or wider, within the bound.
A program may use at most 128 MiB of HBM per device.

v0:
```python
import math
import jax
import jax.numpy as jnp
from jax import lax
from jax.sharding import PartitionSpec as P

GW = 16


def extended_2(cells, sides, width):
    for axis, dim in sides:
        count = lax.axis_size(axis)
        ends = count - 1
        head = lax.slice_in_dim(cells, 0, width, axis=dim)
        tail = lax.slice_in_dim(cells, cells.shape[dim] - width, cells.shape[dim], axis=dim)
        cells = jnp.concatenate(
            [
                lax.ppermute(tail, axis, [(i, (i + 1) % count) for i in range(ends)]),
                cells,
                lax.ppermute(head, axis, [((i + 1) % count, i) for i in range(ends)]),
            ],
            axis=dim,
        )
    return cells


def silu_slope(preact):
    sigmoid_value = jax.nn.sigmoid(preact)
    return sigmoid_value * (1.0 + preact * (1.0 - sigmoid_value))


def block_kernel(full_group, hidden_width, group_width):
    sub_width = min(hidden_width, 128)
    sections = hidden_width // sub_width
    members = sub_width // group_width
    arranged = full_group.reshape(9, group_width, sections, members, group_width)
    arranged = arranged.transpose(0, 2, 3, 1, 4)
    identity = jnp.eye(members, dtype=full_group.dtype)
    expanded = arranged[:, :, :, :, None, :] * identity[None, None, :, None, :, None]
    return expanded.reshape(9, sections, sub_width, sub_width)


def grouped_taps(padded, kernel, out_rows, out_cols, flipped, pattern):
    summed = None
    for tap_index in range(9):
        row_step = tap_index // 3
        col_step = tap_index % 3
        if flipped:
            row_step = 2 - row_step
            col_step = 2 - col_step
        window = padded[:, row_step : row_step + out_rows, col_step : col_step + out_cols, :]
        window = window.reshape(-1, kernel.shape[1], kernel.shape[2])
        tap_term = jnp.einsum(
            pattern, window, kernel[tap_index], preferred_element_type=jnp.float32
        )
        summed = tap_term if summed is None else summed + tap_term
    return summed


def body(images, cotangent, weight_in, weight_group, weight_out):
    tile_count, height, across, channels = images.shape
    block_count = weight_in.shape[0]
    group_width = GW
    pixels = tile_count * height * across
    current = images.reshape(pixels, channels)
    stored = []
    for block_index in range(block_count):
        full_in, full_group, full_out = (
            lax.all_gather(weight_in[block_index], "shard", axis=0, tiled=True),
            lax.all_gather(weight_group[block_index], "shard", axis=0, tiled=True),
            lax.all_gather(weight_out[block_index], "shard", axis=0, tiled=True),
        )
        hidden_width = full_in.shape[1]
        kernel = block_kernel(full_group, hidden_width, group_width)
        pre_one = jnp.dot(current, full_in, preferred_element_type=jnp.float32)
        hidden_one = (
            jax.nn.silu(pre_one)
            .astype(jnp.bfloat16)
            .reshape(tile_count, height, across, hidden_width)
        )
        haloed = extended_2(hidden_one, (("rows", 1),), 1)
        padded_one = jnp.pad(haloed, ((0, 0), (0, 0), (1, 1), (0, 0)))
        pre_two = grouped_taps(padded_one, kernel, height, across, False, "psi,sio->pso").reshape(
            pixels, hidden_width
        )
        hidden_two = jax.nn.silu(pre_two).astype(jnp.bfloat16)
        pre_three = current.astype(jnp.float32) + jnp.dot(
            hidden_two, full_out, preferred_element_type=jnp.float32
        )
        kept_weights = None
        stored.append((current, pre_one, padded_one, pre_two, hidden_two, pre_three, kept_weights))
        current = jax.nn.silu(pre_three).astype(jnp.bfloat16)
    decoded = current.reshape(images.shape)
    grad_flow = cotangent.reshape(pixels, channels)
    shares = []
    for block_index in reversed(range(block_count)):
        flow_in, pre_one, padded_one, pre_two, hidden_two, pre_three, kept_weights = stored[
            block_index
        ]
        full_in, full_group, full_out = (
            lax.all_gather(weight_in[block_index], "shard", axis=0, tiled=True),
            lax.all_gather(weight_group[block_index], "shard", axis=0, tiled=True),
            lax.all_gather(weight_out[block_index], "shard", axis=0, tiled=True),
        )
        hidden_width = full_in.shape[1]
        kernel = block_kernel(full_group, hidden_width, group_width)
        sections = kernel.shape[1]
        sub_width = kernel.shape[2]
        members = sub_width // group_width
        slope_three = grad_flow.astype(jnp.float32) * silu_slope(pre_three)
        low_three = slope_three.astype(jnp.bfloat16)
        part_out = jnp.einsum(
            "pw,pc->wc", hidden_two, low_three, preferred_element_type=jnp.float32
        )
        slope_two = (
            jnp.einsum("pc,wc->pw", low_three, full_out, preferred_element_type=jnp.float32)
            * silu_slope(pre_two)
        ).astype(jnp.bfloat16)
        slope_sections = slope_two.reshape(pixels, sections, sub_width)
        tap_terms = []
        for tap_index in range(9):
            row_step = tap_index // 3
            col_step = tap_index % 3
            window = padded_one[:, row_step : row_step + height, col_step : col_step + across, :]
            window = window.reshape(pixels, sections, sub_width)
            blockwise = jnp.einsum(
                "psi,pso->sio", window, slope_sections, preferred_element_type=jnp.float32
            )
            blockwise = blockwise.reshape(sections, members, group_width, members, group_width)
            diagonal_part = jnp.diagonal(blockwise, axis1=1, axis2=3)
            tap_terms.append(diagonal_part.transpose(1, 0, 3, 2).reshape(group_width, hidden_width))
        part_group = jnp.stack(tap_terms).reshape(9 * group_width, hidden_width)
        slope_grid = slope_two.reshape(tile_count, height, across, hidden_width)
        padded_slope = jnp.pad(slope_grid, ((0, 0), (2, 2), (1, 1), (0, 0)))
        extended = grouped_taps(padded_slope, kernel, height + 2, across, True, "pso,sio->psi")
        extended = extended.reshape(tile_count, height + 2, across, hidden_width)
        edge_rows = jnp.concatenate([extended[:, :1], extended[:, -1:]], axis=1)
        borders = extended_2(edge_rows.astype(jnp.bfloat16), (("rows", 1),), 1).astype(
            edge_rows.dtype
        )
        back_one = extended[:, 1:-1]
        back_one = back_one.at[:, :1].add(borders[:, :1])
        back_one = back_one.at[:, -1:].add(borders[:, -1:])
        slope_one = (back_one.reshape(pixels, hidden_width) * silu_slope(pre_one)).astype(
            jnp.bfloat16
        )
        part_in = jnp.einsum("pc,pw->cw", flow_in, slope_one, preferred_element_type=jnp.float32)
        grad_flow = (
            slope_three
            + jnp.einsum("pw,cw->pc", slope_one, full_in, preferred_element_type=jnp.float32)
        ).astype(jnp.bfloat16)
        shares.append(
            (
                lax.psum_scatter(
                    part_in.astype(jnp.bfloat16), "shard", scatter_dimension=0, tiled=True
                ).astype(jnp.float32),
                lax.psum_scatter(
                    part_group.astype(jnp.bfloat16), "shard", scatter_dimension=0, tiled=True
                ).astype(jnp.float32),
                lax.psum_scatter(
                    part_out.astype(jnp.bfloat16), "shard", scatter_dimension=0, tiled=True
                ).astype(jnp.float32),
            )
        )
    shares = shares[::-1]
    totals = (
        lax.psum(jnp.stack([entry[0] for entry in shares]).astype(jnp.bfloat16), "rows").astype(
            jnp.float32
        ),
        lax.psum(jnp.stack([entry[1] for entry in shares]).astype(jnp.bfloat16), "rows").astype(
            jnp.float32
        ),
        lax.psum(jnp.stack([entry[2] for entry in shares]).astype(jnp.bfloat16), "rows").astype(
            jnp.float32
        ),
    )
    norm_factor = 1.0 / math.sqrt(pixels * lax.axis_size("rows") * lax.axis_size("shard"))
    grad_images = grad_flow.reshape(images.shape)
    return (
        decoded,
        grad_images,
        totals[0] * norm_factor,
        totals[1] * norm_factor,
        totals[2] * norm_factor,
    )


def solution(mesh):
    placed = (
        P(("groups", "shard"), "rows", None, None),
        P(("groups", "shard"), "rows", None, None),
        P(None, "shard", None),
        P(None, "shard", None),
        P(None, "shard", None),
    )
    return jax.shard_map(
        body,
        mesh=mesh,
        in_specs=placed,
        out_specs=(
            P(("groups", "shard"), "rows", None, None),
            P(("groups", "shard"), "rows", None, None),
            P("groups", "shard", None),
            P("groups", "shard", None),
            P("groups", "shard", None),
        ),
        check_vma=False,
    )
```

profile of v0, /device:TPU:0, one launch (start us, length us, event | category | flops | bytes accessed | tf_op | source)
XLA Modules:
  0.0 434.7 jit_solution(18209110213923368101)
XLA Ops:
  7.2 1.7 fusion.117
  8.9 8.6 %all-gather.1 = bf16[1,512,512]{2,1,0:T(8,128)(2,1)S(1)} all-gather(bf16[1,128,512]{2,1,0:T(8,128)(2,1)S(1)} %get-tuple-element.137), channel_id=3, replica_groups=mesh['groups'=2,'rows'=4,'shard'=4] {'shard'}, dimensions={1}, use_global_device_ids=true | all-gather | bytes 655360 | tf_op jit(solution)/shard_map/all_gather | solution.py:69
  20.6 5.2 %collective-permute-start = (bf16[1,1,128,512]{3,2,1,0:T(8,128)(2,1)}, bf16[1,1,128,512]{3,2,1,0:T(8,128)(2,1)}, u32[]{:S(2)}, u32[]{:S(2)}) collective-permute-start(bf16[1,1,128,512]{3,2,1,0:T(8,128)(2,1)} %get-tuple-element.135), channel_id=1, source_target_pairs={{0,4},{4,8},{8,12},{1,5},{5,9},{9,13},{2,6},{6,10},{10,14},{3,7},{... | collective-permute-start | bytes 393224 | tf_op jit(solution)/shard_map/ppermute | solution.py:18
  27.5 5.9 %all-gather = bf16[1,144,512]{2,0,1:T(2,128)(2,1)S(1)} all-gather(bf16[1,36,512]{2,0,1:T(2,128)(2,1)S(1)} %get-tuple-element.141), channel_id=2, replica_groups=mesh['groups'=2,'rows'=4,'shard'=4] {'shard'}, dimensions={1}, use_global_device_ids=true | all-gather | bytes 184320 | tf_op jit(solution)/shard_map/all_gather | solution.py:70
  36.6 6.0 %all-gather.3 = bf16[1,144,512]{2,0,1:T(2,128)(2,1)S(1)} all-gather(bf16[1,36,512]{2,0,1:T(2,128)(2,1)S(1)} %get-tuple-element.142), channel_id=5, replica_groups=mesh['groups'=2,'rows'=4,'shard'=4] {'shard'}, dimensions={1}, use_global_device_ids=true | all-gather | bytes 184320 | tf_op jit(solution)/shard_map/all_gather | solution.py:70
  45.9 9.3 %all-gather.4 = bf16[1,512,512]{2,1,0:T(8,128)(2,1)} all-gather(bf16[1,128,512]{2,1,0:T(8,128)(2,1)} %get-tuple-element.138), channel_id=6, replica_groups=mesh['groups'=2,'rows'=4,'shard'=4] {'shard'}, dimensions={1}, use_global_device_ids=true | all-gather | bytes 655360 | tf_op jit(solution)/shard_map/all_gather | solution.py:69
  55.2 4.4 %broadcast_multiply_fusion.1 = (bf16[9,4,8,16,8,16]{3,2,5,4,1,0:T(8,128)(2,1)S(1)}, bf16[9,4,8,16,8,16]{3,2,5,4,1,0:T(8,128)(2,1)}) fusion(bf16[8,8]{0,1:T(8,128)(2,1)S(1)} %fusion.107, bf16[9,4,8,16,16]{3,2,4,1,0:T(8,128)(2,1)S(1)} %copy.227, bf16[9,4,8,16,16]{3,2,4,1,0:T(8,128)(2,1)S(1)} %copy.238), kind=kLoop, calls=%fused_computation.19 | loop fusion | flops 1179648 | bytes 2654336 | tf_op jit(solution)/shard_map/mul | solution.py:39
  59.6 9.0 %fusion.109 = (bf16[1,4,8,16,8,16]{3,2,5,4,1,0:T(8,128)(2,1)S(1)}, bf16[1,4,8,16,8,16]{3,2,5,4,1,0:T(8,128)(2,1)S(1)}, bf16[1,4,8,16,8,16]{3,2,5,4,1,0:T(8,128)(...) fusion(bf16[9,4,8,16,8,16]{3,2,5,4,1,0:T(8,128)(2,1)} %get-tupl, ...), kind=kLoop, calls=%fused_computation.285 | loop fusion | bytes 4718592 | tf_op jit(solution)/shard_map/slice | solution.py:54
  68.6 2.0 squeeze.97
  70.6 2.6 squeeze.99
  73.2 2.6 squeeze.100
  75.9 2.6 squeeze.101
  78.5 2.6 squeeze.102
  81.1 2.6 squeeze.103
  83.7 2.6 squeeze.104
  86.3 2.6 squeeze.105
  88.9 2.6 squeeze.106
  91.5 8.8 %all-gather.2 = bf16[1,512,512]{2,1,0:T(8,128)(2,1)} all-gather(bf16[1,128,512]{2,1,0:T(8,128)(2,1)} %get-tuple-element.139), channel_id=4, replica_groups=mesh['groups'=2,'rows'=4,'shard'=4] {'shard'}, dimensions={1}, use_global_device_ids=true | all-gather | bytes 655360 | tf_op jit(solution)/shard_map/all_gather | solution.py:71
  102.6 1.7 reshape.625
  104.4 1.8 copy.294
  106.2 1.8 pad_maximum_fusion.2
  108.0 1.8 reshape.626
  109.8 1.8 copy.298
  112.4 1.8 copy.302
  114.2 1.8 reshape.628
  116.0 1.8 copy.306
  117.8 1.7 reshape.630
  119.5 1.8 copy.314
  122.1 1.8 copy.318
  123.9 1.8 reshape.632
  125.7 1.8 copy.322
  127.5 1.7 reshape.633
  129.2 1.8 copy.326
  136.6 2.1 copy.389
  138.7 1.6 convolution_add_fusion.35
  143.5 5.2 %collective-permute-start.2 = (bf16[1,1,128,512]{3,2,1,0:T(8,128)(2,1)}, bf16[1,1,128,512]{3,2,1,0:T(8,128)(2,1)}, u32[]{:S(2)}, u32[]{:S(2)}) collective-permute-start(bf16[1,1,128,512]{3,2,1,0:T(8,128)(2,1)} %get-tuple-element.131), channel_id=1, source_target_pairs={{0,4},{4,8},{8,12},{1,5},{5,9},{9,13},{2,6},{6,10},{10,14},{3,7},{... | collective-permute-start | bytes 393224 | tf_op jit(solution)/shard_map/ppermute | solution.py:18
  148.7 7.2 %all-gather.5 = bf16[1,512,512]{2,1,0:T(8,128)(2,1)} all-gather(bf16[1,128,512]{2,1,0:T(8,128)(2,1)S(1)} %copy-done.92), channel_id=7, replica_groups=mesh['groups'=2,'rows'=4,'shard'=4] {'shard'}, dimensions={1}, use_global_device_ids=true | all-gather | bytes 655360 | tf_op jit(solution)/shard_map/all_gather | solution.py:71
  155.9 2.6 squeeze.109
  158.5 2.6 squeeze.111
  161.1 2.6 squeeze.112
  163.7 2.6 squeeze.113
  166.3 2.6 squeeze.114
  168.9 2.8 squeeze.115
  186.2 2.7 convert_multiply_fusion
  198.2 1.7 pad_slice_fusion.9
  202.3 2.0 reshape.650
  204.3 2.0 reshape.651
  206.2 2.0 reshape.652
  208.2 1.9 reshape.653
  212.9 1.5 convolution_add_fusion.15
  223.7 5.2 %collective-permute-start.4 = (bf16[1,1,128,512]{3,2,1,0:T(8,128)(2,1)}, bf16[1,1,128,512]{3,2,1,0:T(8,128)(2,1)}, u32[]{:S(2)}, u32[]{:S(2)}) collective-permute-start(bf16[1,1,128,512]{3,2,1,0:T(8,128)(2,1)} %copy.401), channel_id=1, source_target_pairs={{0,4},{4,8},{8,12},{1,5},{5,9},{9,13},{2,6},{6,10},{10,14},{3,7},{... | collective-permute-start | bytes 393224 | tf_op jit(solution)/shard_map/ppermute | solution.py:18
  264.3 1.6 pad_slice_fusion
  268.3 2.0 reshape.662
  270.2 2.0 reshape.663
  272.2 2.0 reshape.664
  274.2 2.0 reshape.665
  279.0 1.5 convolution_add_fusion.7
  291.5 5.4 %collective-permute-start.6 = (bf16[1,1,128,512]{3,2,1,0:T(8,128)(2,1)}, bf16[1,1,128,512]{3,2,1,0:T(8,128)(2,1)}, u32[]{:S(2)}, u32[]{:S(2)}) collective-permute-start(bf16[1,1,128,512]{3,2,1,0:T(8,128)(2,1)} %copy.405), channel_id=1, source_target_pairs={{0,4},{4,8},{8,12},{1,5},{5,9},{9,13},{2,6},{6,10},{10,14},{3,7},{... | collective-permute-start | bytes 393224 | tf_op jit(solution)/shard_map/ppermute | solution.py:18
  308.0 2.3 convolution_convert_fusion.2
  330.3 8.6 %fusion.108 = (bf16[40,512]{1,0:T(8,128)(2,1)S(1)}, bf16[40,512]{1,0:T(8,128)(2,1)S(1)}) fusion(bf16[144,512]{1,0:T(8,128)(2,1)} %bitcast.72, bf16[144,512]{1,0:T(8,128)(2,1)S(1)} %bitcast.611), kind=kCustom, calls=%all-reduce-scatter.2 | all-reduce-scatter fusion | flops 163841 | bytes 377344
  340.3 3.7 collective-permute-start.8
  348.4 7.7 %reduce-scatter.21.cloned.1.call-done = bf16[128,512]{1,0:T(8,128)(2,1)} async-done(((bf16[512,512]{1,0:T(8,128)(2,1)}), bf16[128,512]{1,0:T(8,128)(2,1)}) %reduce-scatter.21.cloned.1.call-update) | async-done | bytes 131088
  357.9 23.0 %reduce-scatter.17.cloned.1.call-done = bf16[128,512]{1,0:T(8,128)(2,1)} async-done(((bf16[512,512]{1,0:T(8,128)(2,1)}), bf16[128,512]{1,0:T(8,128)(2,1)}) %reduce-scatter.17.cloned.1.call-update) | async-done | bytes 131088
  383.8 40.3 %all-reduce.12.cloned.1.call-done = (bf16[2,128,512]{1,2,0:T(8,128)(2,1)}, bf16[2,36,512]{2,1,0:T(8,128)(2,1)}, bf16[2,128,512]{1,2,0:T(8,128)(2,1)}) async-done(((bf16[2,128,512]{1,2,0:T(8,128)(2,1)}, bf16[2,36,512]{2,1,0:T(8,128)(2,1)}, bf16[2,128,512]{1,2,0:T(8,128)(2,1)}), (bf16[2,128,512]{1,2,0:T(8,128)(2,1)}, bf16[2,36,512]{2,1,0:T(8,128)(2,1)}, ...) | async-done | bytes 598032 | tf_op jit(solution)/shard_map/psum | solution.py:167
  (538 shorter events, 156.2 us)
Async XLA Ops:
  7.2 10.3 %copy-start.98 = (bf16[1,2,128,512]{3,2,1,0:T(8,128)(2,1)S(1)}, bf16[1,2,128,512]{3,2,1,0:T(8,128)(2,1)}, u32[]{:S(2)}) copy-start(bf16[1,2,128,512]{3,2,1,0:T(8,128)(2,1)} %param.13) | copy-start | bytes 786436
  7.2 339.2 %reduce-scatter.23.cloned.1.call-start = ((), (), s32[]{:S(2)}) async-start(), calls=%async_computation.7 | async-start | bytes 655360
  18.6 14.8 %copy-start = (bf16[256,512]{1,0:T(8,128)(2,1)}, bf16[256,512]{1,0:T(8,128)(2,1)S(1)}, u32[]{:S(2)}) copy-start(bf16[256,512]{1,0:T(8,128)(2,1)S(1)} %get-tuple-element.145) | copy-start | bytes 786436
  18.6 8.1 %copy-start.97 = (bf16[2,128,512]{2,1,0:T(8,128)(2,1)S(1)}, bf16[2,128,512]{2,1,0:T(8,128)(2,1)}, u32[]{:S(2)}) copy-start(bf16[2,128,512]{2,1,0:T(8,128)(2,1)} %param.17) | copy-start | bytes 786436
  18.6 8.8 %copy-start.93 = (bf16[2,36,512]{2,0,1:T(2,128)(2,1)S(1)}, bf16[2,36,512]{2,0,1:T(2,128)(2,1)}, u32[]{:S(2)}) copy-start(bf16[2,36,512]{2,0,1:T(2,128)(2,1)} %param.16) | copy-start | bytes 221188
  19.3 81.0 %collective-permute-start.1 = (bf16[1,1,128,512]{3,2,1,0:T(8,128)(2,1)}, bf16[1,1,128,512]{3,2,1,0:T(8,128)(2,1)}, u32[]{:S(2)}, u32[]{:S(2)}) collective-permute-start(bf16[1,1,128,512]{3,2,1,0:T(8,128)(2,1)} %get-tuple-element.136), channel_id=1, source_target_pairs={{4,0},{8,4},{12,8},{5,1},{9,5},{13,9},{6,2},{10,6},{14,10},{7,3},{... | collective-permute-start | bytes 393224 | tf_op jit(solution)/shard_map/ppermute | solution.py:20
  20.6 79.7 %collective-permute-start = (bf16[1,1,128,512]{3,2,1,0:T(8,128)(2,1)}, bf16[1,1,128,512]{3,2,1,0:T(8,128)(2,1)}, u32[]{:S(2)}, u32[]{:S(2)}) collective-permute-start(bf16[1,1,128,512]{3,2,1,0:T(8,128)(2,1)} %get-tuple-element.135), channel_id=1, source_target_pairs={{0,4},{4,8},{8,12},{1,5},{5,9},{9,13},{2,6},{6,10},{10,14},{3,7},{... | collective-permute-start | bytes 393224 | tf_op jit(solution)/shard_map/ppermute | solution.py:18
  88.9 11.5 %copy-start.1 = (bf16[256,512]{1,0:T(8,128)(2,1)S(1)}, bf16[256,512]{1,0:T(8,128)(2,1)}, u32[]{:S(2)}) copy-start(bf16[256,512]{1,0:T(8,128)(2,1)} %copy-done) | copy-start | bytes 786436
  108.0 3.6 copy-start.63
  114.2 7.1 %copy-start.62 = (bf16[1,2,128,512]{3,2,1,0:T(8,128)(2,1)S(1)}, bf16[1,2,128,512]{3,2,1,0:T(8,128)(2,1)}, u32[]{:S(2)}) copy-start(bf16[1,2,128,512]{3,2,1,0:T(8,128)(2,1)} %get-tuple-element.104) | copy-start | bytes 786436
  123.9 7.1 %copy-start.2 = (bf16[256,4,128]{0,2,1:T(8,128)(2,1)S(1)}, bf16[256,4,128]{0,2,1:T(8,128)(2,1)}, u32[]{:S(2)}) copy-start(bf16[256,4,128]{0,2,1:T(8,128)(2,1)} %copy.294) | copy-start | bytes 786436
  140.3 8.4 %copy-start.92 = (bf16[1,128,512]{2,1,0:T(8,128)(2,1)S(1)}, bf16[1,128,512]{2,1,0:T(8,128)(2,1)}, u32[]{:S(2)}) copy-start(bf16[1,128,512]{2,1,0:T(8,128)(2,1)} %get-tuple-element.140) | copy-start | bytes 393220
  142.2 33.0 %collective-permute-start.3 = (bf16[1,1,128,512]{3,2,1,0:T(8,128)(2,1)}, bf16[1,1,128,512]{3,2,1,0:T(8,128)(2,1)}, u32[]{:S(2)}, u32[]{:S(2)}) collective-permute-start(bf16[1,1,128,512]{3,2,1,0:T(8,128)(2,1)} %get-tuple-element.132), channel_id=1, source_target_pairs={{4,0},{8,4},{12,8},{5,1},{9,5},{13,9},{6,2},{10,6},{14,10},{7,3},{... | collective-permute-start | bytes 393224 | tf_op jit(solution)/shard_map/ppermute | solution.py:20
  143.5 31.8 %collective-permute-start.2 = (bf16[1,1,128,512]{3,2,1,0:T(8,128)(2,1)}, bf16[1,1,128,512]{3,2,1,0:T(8,128)(2,1)}, u32[]{:S(2)}, u32[]{:S(2)}) collective-permute-start(bf16[1,1,128,512]{3,2,1,0:T(8,128)(2,1)} %get-tuple-element.131), channel_id=1, source_target_pairs={{0,4},{4,8},{8,12},{1,5},{5,9},{9,13},{2,6},{6,10},{10,14},{3,7},{... | collective-permute-start | bytes 393224 | tf_op jit(solution)/shard_map/ppermute | solution.py:18
  173.7 10.5 %copy-start.48 = (bf16[4,128,128]{1,2,0:T(8,128)(2,1)}, bf16[4,128,128]{1,2,0:T(8,128)(2,1)S(1)}, u32[]{:S(2)}) copy-start(bf16[4,128,128]{1,2,0:T(8,128)(2,1)S(1)} %squeeze.117) | copy-start | bytes 393220
  179.1 2.2 copy-start.31
  179.4 2.1 copy-start.60
  186.2 2.8 copy-start.86
  186.2 2.8 copy-start.91
  188.9 8.2 %copy-start.119 = (f32[256,512]{1,0:T(8,128)}, f32[256,512]{1,0:T(8,128)S(1)}, u32[]{:S(2)}) copy-start(f32[256,512]{1,0:T(8,128)S(1)} %get-tuple-element.109) | copy-start | bytes 1572868
  221.0 7.8 %copy-start.76 = (bf16[4,128,128]{2,1,0:T(8,128)(2,1)S(1)}, bf16[4,128,128]{2,1,0:T(8,128)(2,1)}, u32[]{:S(2)}) copy-start(bf16[4,128,128]{2,1,0:T(8,128)(2,1)} %fusion.61) | copy-start | bytes 393220
  221.6 35.3 %collective-permute-start.5 = (bf16[1,1,128,512]{3,2,1,0:T(8,128)(2,1)S(1)}, bf16[1,1,128,512]{3,2,1,0:T(8,128)(2,1)}, u32[]{:S(2)}, u32[]{:S(2)}) collective-permute-start(bf16[1,1,128,512]{3,2,1,0:T(8,128)(2,1)S(1)} %copy.402), channel_id=1, source_target_pairs={{4,0},{8,4},{12,8},{5,1},{9,5},{13,9},{6,2},{10,6},{14,10},{7,3},{... | collective-permute-start | bytes 393224 | tf_op jit(solution)/shard_map/ppermute | solution.py:20
  223.7 33.2 %collective-permute-start.4 = (bf16[1,1,128,512]{3,2,1,0:T(8,128)(2,1)}, bf16[1,1,128,512]{3,2,1,0:T(8,128)(2,1)}, u32[]{:S(2)}, u32[]{:S(2)}) collective-permute-start(bf16[1,1,128,512]{3,2,1,0:T(8,128)(2,1)} %copy.401), channel_id=1, source_target_pairs={{0,4},{4,8},{8,12},{1,5},{5,9},{9,13},{2,6},{6,10},{10,14},{3,7},{... | collective-permute-start | bytes 393224 | tf_op jit(solution)/shard_map/ppermute | solution.py:18
  229.5 1.7 copy-start.74
  231.9 1.7 copy-start.73
  236.7 1.7 copy-start.71
  241.5 1.7 copy-start.69
  243.9 1.7 copy-start.68
  248.9 1.8 copy-start.105
  248.9 2.4 copy-start.107
  248.9 3.0 copy-start.109
  248.9 3.6 copy-start.110
  248.9 4.2 copy-start.112
  248.9 4.8 %copy-start.114 = (bf16[1,16,512]{2,1,0:T(8,128)(2,1)S(1)}, bf16[1,16,512]{2,1,0:T(8,128)(2,1)}, u32[]{:S(2)}) copy-start(bf16[1,16,512]{2,1,0:T(8,128)(2,1)} %stack_reshape.88) | copy-start | bytes 49156
  249.8 97.5 %reduce-scatter.19.cloned.1.call-start = ((), (), s32[]{:S(2)}) async-start(), calls=%async_computation.5 | async-start | bytes 655360
  256.8 2.2 copy-start.90
  260.6 2.0 copy-start.16
  261.7 1.7 copy-start.18
  287.2 9.7 %copy-start.78 = (bf16[4,128,128]{2,1,0:T(8,128)(2,1)S(1)}, bf16[4,128,128]{2,1,0:T(8,128)(2,1)}, u32[]{:S(2)}) copy-start(bf16[4,128,128]{2,1,0:T(8,128)(2,1)} %fusion.79) | copy-start | bytes 393220
  289.5 37.1 %collective-permute-start.7 = (bf16[1,1,128,512]{3,2,1,0:T(8,128)(2,1)}, bf16[1,1,128,512]{3,2,1,0:T(8,128)(2,1)}, u32[]{:S(2)}, u32[]{:S(2)}) collective-permute-start(bf16[1,1,128,512]{3,2,1,0:T(8,128)(2,1)} %copy.406), channel_id=1, source_target_pairs={{4,0},{8,4},{12,8},{5,1},{9,5},{13,9},{6,2},{10,6},{14,10},{7,3},{... | collective-permute-start | bytes 393224 | tf_op jit(solution)/shard_map/ppermute | solution.py:20
  291.5 35.1 %collective-permute-start.6 = (bf16[1,1,128,512]{3,2,1,0:T(8,128)(2,1)}, bf16[1,1,128,512]{3,2,1,0:T(8,128)(2,1)}, u32[]{:S(2)}, u32[]{:S(2)}) collective-permute-start(bf16[1,1,128,512]{3,2,1,0:T(8,128)(2,1)} %copy.405), channel_id=1, source_target_pairs={{0,4},{4,8},{8,12},{1,5},{5,9},{9,13},{2,6},{6,10},{10,14},{3,7},{... | collective-permute-start | bytes 393224 | tf_op jit(solution)/shard_map/ppermute | solution.py:18
  300.0 1.7 copy-start.75
  305.0 1.9 copy-start.5
  305.0 2.1 copy-start.13
  305.6 2.4 copy-start.95
  308.0 2.4 copy-start.113
  308.0 2.4 copy-start.115
  308.0 2.4 copy-start.7
  310.3 1.9 copy-start.11
  310.3 2.1 copy-start.65
  310.3 45.9 %reduce-scatter.21.cloned.1.call-start = ((), (), s32[]{:S(2)}) async-start(), calls=%async_computation.6 | async-start | bytes 655360
  310.4 2.0 copy-start.89
  315.2 1.7 copy-start.79
  317.6 1.7 copy-start.82
  325.9 2.7 copy-start.87
  325.9 55.0 %reduce-scatter.17.cloned.1.call-start = ((), (), s32[]{:S(2)}) async-start(), calls=%async_computation.4 | async-start | bytes 655360
  329.2 14.9 %copy-start.117 = (u32[32]{0:T(128)S(1)}, u32[32]{0:T(128)}, u32[]{:S(2)}) copy-start(u32[32]{0:T(128)} %constant.395) | copy-start | bytes 388
  330.2 93.8 %all-reduce.12.cloned.1.call-start = ((), (), s32[]{:S(2)}) async-start(), calls=%async_computation.8 | async-start | bytes 1212416 | tf_op jit(solution)/shard_map/psum | solution.py:167
  339.0 6.3 %collective-permute-start.9 = (bf16[12,512]{1,0:T(8,128)(2,1)S(1)}, bf16[12,512]{1,0:T(8,128)(2,1)S(1)}, u32[]{:S(2)}, u32[]{:S(2)}) collective-permute-start(bf16[12,512]{1,0:T(8,128)(2,1)S(1)} %slice.573), channel_id=1, source_target_pairs={{0,1},{1,2},{2,3},{4,5},{5,6},{6,7},{8,9},{9,10},{10,11},{12,13},{... | collective-permute-start | bytes 36872
  340.3 5.1 %collective-permute-start.8 = (bf16[12,512]{1,0:T(8,128)(2,1)S(1)}, bf16[12,512]{1,0:T(8,128)(2,1)S(1)}, u32[]{:S(2)}, u32[]{:S(2)}) collective-permute-start(bf16[12,512]{1,0:T(8,128)(2,1)S(1)} %slice.572), channel_id=1, source_target_pairs={{0,1},{1,2},{2,3},{4,5},{5,6},{6,7},{8,9},{9,10},{10,11},{12,13},{... | collective-permute-start | bytes 36872
  348.4 34.3 %copy-start.20 = (bf16[1,512,512]{2,1,0:T(8,128)(2,1)S(1)}, bf16[1,512,512]{2,1,0:T(8,128)(2,1)}, u32[]{:S(2)}) copy-start(bf16[1,512,512]{2,1,0:T(8,128)(2,1)} %copy-done.19) | copy-start | bytes 1572868
  348.4 34.3 %copy-start.66 = (f32[256,512]{1,0:T(8,128)S(1)}, f32[256,512]{1,0:T(8,128)}, u32[]{:S(2)}) copy-start(f32[256,512]{1,0:T(8,128)} %copy-done.64) | copy-start | bytes 1572868
  424.0 2.0 copy-start.102
  424.0 2.8 copy-start.96
  (74 other events, 86.5 us)
Sparse Core Ops, SparseCore 0:
  250.0 21.4 reduce-scatter.22
  310.4 21.4 reduce-scatter.18
  334.5 21.6 reduce-scatter.20
  359.2 21.6 reduce-scatter.16
  383.9 40.0 all-reduce.11
where the time goes:
time: 443 us; the launch traced here: 435 us
  local copies, waits for them, and re-layouts  196 us (44%)
  waiting for transfers between devices  71.1 us (16%)
  blocking collectives  54.5 us (12%)
  matrix products  44.2 us (10%)
  starting transfers between devices  31.5 us (7%)
  other arithmetic  20.9 us (5%)
  between operations  16.9 us (4%)
    reshape x52, local copies, waits for them, and re-layouts, grouped_taps(): window = window.reshape(-1, kernel.shape[1], kernel.shape[2])  52.9 us
    squeeze x18, local copies, waits for them, and re-layouts, grouped_taps(): kernel[tap_index]  42 us
    psum x1, waiting for transfers between devices, body(): lax.psum(jnp.stack([entry[0] for entry in shares]).astype(jnp.bfloat16),...  40.3 us
    unnamed x283, local copies, waits for them, and re-layouts  31.7 us
    unnamed x11, waiting for transfers between devices  30.8 us
    ppermute x4, starting transfers between devices, extended_2(): lax.ppermute(tail, axis, [(i, (i + 1) % count) for i in range(ends)])  21 us
    all_gather x2, blocking collectives, body(): lax.all_gather(weight_in[block_index], 'shard', axis=0, tiled=True)  17.9 us
    dot_general x36, matrix products, grouped_taps(): jnp.einsum(pattern, window, kernel[tap_index], preferred_element_type=jnp...  16.2 us
  transfers between devices with their start and end apart: 15, of which 3 were waited for; matrix products, arithmetic and copies ran while one was open for 38% of the time, Pallas kernels for 0%

commit v1 on v0

--- a/solution.py
+++ b/solution.py
@@ -5,6 +5,27 @@
 from jax.sharding import PartitionSpec as P
 
 GW = 16
+
+
+def ring_gather(shard, axis, dim):
+    length, here, span = (lax.axis_size(axis), lax.axis_index(axis), shard.shape[dim])
+    forward = [(i, (i + 1) % length) for i in range(length)]
+    behind = [(i, (i - 1) % length) for i in range(length)]
+    out = jnp.zeros((*shard.shape[:dim], length * span, *shard.shape[dim + 1 :]), shard.dtype)
+    out = lax.dynamic_update_slice_in_dim(out, shard, here * span, axis=dim)
+    from_left = from_right = shard
+    halfway = length // 2
+    for hop in range(1, halfway + 1):
+        from_left = lax.ppermute(from_left, axis, forward)
+        out = lax.dynamic_update_slice_in_dim(
+            out, from_left, (here - hop) % length * span, axis=dim
+        )
+        if hop < length - halfway:
+            from_right = lax.ppermute(from_right, axis, behind)
+            out = lax.dynamic_update_slice_in_dim(
+                out, from_right, (here + hop) % length * span, axis=dim
+            )
+    return out
 
 
 def extended_2(cells, sides, width):
@@ -66,7 +87,7 @@
     stored = []
     for block_index in range(block_count):
         full_in, full_group, full_out = (
-            lax.all_gather(weight_in[block_index], "shard", axis=0, tiled=True),
+            ring_gather(weight_in[block_index], "shard", 0),
             lax.all_gather(weight_group[block_index], "shard", axis=0, tiled=True),
             lax.all_gather(weight_out[block_index], "shard", axis=0, tiled=True),
         )

time: 443 us -> 488 us (1.10)
  local copies, waits for them, and re-layouts: 196 us -> 253 us
  waiting for transfers between devices: 71.1 us -> 55.7 us
    gather x18, local copies, waits for them, and re-layouts: 10.7 us -> 32.7 us  [body(): diagonal_part = jnp.diagonal(blockwise, axis1=1, axis2=3)]
    reshape x36, local copies, waits for them, and re-layouts: 15.9 us -> 34.5 us  [body(): blockwise.reshape(sections, members, group_width, members, group_width)]
    unnamed x11, waiting for transfers between devices: 30.8 us -> 21.9 us
    dynamic_update_slice x0 -> x8, local copies, waits for them, and re-layouts: none -> 8.71 us  [the longest x4 4.89 us: ring_gather(): lax.dynamic_update_slice_in_dim(out, from_left, (here - hop) % length * s...]
    another operation x20, local copies, waits for them, and re-layouts: 12.3 us -> 4.48 us  [body(): part_group = jnp.stack(tap_terms).reshape(9 * group_width, hidden_width)]
    psum x1, waiting for transfers between devices: 40.3 us -> 32.6 us  [body(): lax.psum(jnp.stack([entry[0] for entry in shares]).astype(jnp.bfloat16),...]
    unnamed x283 -> x269, local copies, waits for them, and re-layouts: 31.7 us -> 38.2 us
    reshape x52 -> x50, local copies, waits for them, and re-layouts: 52.9 us -> 57.8 us  [grouped_taps(): window = window.reshape(-1, kernel.shape[1], kernel.shape[2])]
  transfers between devices with their start and end apart: 15 -> 21, of which waited for: 3 -> 3; matrix products, arithmetic and copies ran while one was open for 38% -> 46% of each run, Pallas kernels for 0% -> 0%
where the time goes in v1:
time: 488 us; the launch traced here: 481 us
  local copies, waits for them, and re-layouts  253 us (52%)
  waiting for transfers between devices  55.7 us (11%)
  blocking collectives  53.5 us (11%)
  matrix products  42.2 us (9%)
  starting transfers between devices  36.1 us (7%)
  other arithmetic  23.6 us (5%)
  between operations  16.7 us (3%)
    reshape x50, local copies, waits for them, and re-layouts, grouped_taps(): window = window.reshape(-1, kernel.shape[1], kernel.shape[2])  57.8 us
    squeeze x18, local copies, waits for them, and re-layouts, grouped_taps(): kernel[tap_index]  44 us
    unnamed x269, local copies, waits for them, and re-layouts  38.2 us
    reshape x36, local copies, waits for them, and re-layouts, body(): blockwise.reshape(sections, members, group_width, members, group_width)  34.5 us
    gather x18, local copies, waits for them, and re-layouts, body(): diagonal_part = jnp.diagonal(blockwise, axis1=1, axis2=3)  32.7 us
    psum x1, waiting for transfers between devices, body(): lax.psum(jnp.stack([entry[0] for entry in shares]).astype(jnp.bfloat16),...  32.6 us
    unnamed x11, waiting for transfers between devices  21.9 us
    ppermute x4, starting transfers between devices, extended_2(): lax.ppermute(tail, axis, [(i, (i + 1) % count) for i in range(ends)])  20.3 us
  transfers between devices with their start and end apart: 21, of which 3 were waited for; matrix products, arithmetic and copies ran while one was open for 46% of the time, Pallas kernels for 0%

profile of v1, /device:TPU:0, one launch (start us, length us, event | category | flops | bytes accessed | tf_op | source)
XLA Modules:
  0.0 480.9 jit_solution(14241513324756811907)
XLA Ops:
  9.4 1.9 collective-permute-start.6
  14.2 7.0 %all-gather = bf16[1,144,512]{2,0,1:T(2,128)(2,1)S(1)} all-gather(bf16[1,36,512]{2,0,1:T(2,128)(2,1)S(1)} %get-tuple-element.145), channel_id=2, replica_groups=mesh['groups'=2,'rows'=4,'shard'=4] {'shard'}, dimensions={1}, use_global_device_ids=true | all-gather | bytes 184320 | tf_op jit(solution)/shard_map/all_gather | solution.py:91
  24.4 6.9 %all-gather.2 = bf16[1,144,512]{2,0,1:T(2,128)(2,1)S(1)} all-gather(bf16[1,36,512]{2,0,1:T(2,128)(2,1)S(1)} %get-tuple-element.146), channel_id=4, replica_groups=mesh['groups'=2,'rows'=4,'shard'=4] {'shard'}, dimensions={1}, use_global_device_ids=true | all-gather | bytes 184320 | tf_op jit(solution)/shard_map/all_gather | solution.py:91
  34.5 4.4 broadcast_multiply_fusion.1
  39.0 9.4 %fusion.62 = (bf16[1,4,8,16,8,16]{3,2,5,4,1,0:T(8,128)(2,1)S(1)}, bf16[1,4,8,16,8,16]{3,2,5,4,1,0:T(8,128)(2,1)S(1)}, bf16[1,4,8,16,8,16]{3,2,5,4,1,0:T(8,128)(2...) fusion(bf16[9,4,8,16,8,16]{3,2,5,4,1,0:T(8,128)(2,1)} %get-tupl, ...), kind=kLoop, calls=%fused_computation.252 | loop fusion | bytes 4718592 | tf_op jit(solution)/shard_map/slice | solution.py:75
  48.4 2.1 squeeze.97
  52.0 2.6 squeeze.99
  54.6 2.6 squeeze.100
  57.2 2.6 squeeze.101
  59.8 2.6 squeeze.102
  62.4 2.6 squeeze.103
  65.0 2.6 squeeze.104
  67.6 2.6 squeeze.105
  70.2 2.6 squeeze.106
  73.6 7.4 %all-gather.1 = bf16[1,512,512]{2,1,0:T(8,128)(2,1)S(1)} all-gather(bf16[1,128,512]{2,1,0:T(8,128)(2,1)S(1)} %get-tuple-element.136), channel_id=3, replica_groups=mesh['groups'=2,'rows'=4,'shard'=4] {'shard'}, dimensions={1}, use_global_device_ids=true | all-gather | bytes 655360 | tf_op jit(solution)/shard_map/all_gather | solution.py:92
  81.9 1.8 bitcast_convert_fusion
  83.7 9.3 %all-gather.3 = bf16[1,512,512]{2,1,0:T(8,128)(2,1)} all-gather(bf16[1,128,512]{2,1,0:T(8,128)(2,1)} %get-tuple-element.135), channel_id=5, replica_groups=mesh['groups'=2,'rows'=4,'shard'=4] {'shard'}, dimensions={1}, use_global_device_ids=true | all-gather | bytes 655360 | tf_op jit(solution)/shard_map/all_gather | solution.py:92
  99.7 2.2 multiply_convert_fusion.5
  103.4 4.6 collective-permute-start.3
  115.5 1.8 pad_maximum_fusion.2
  125.2 1.8 copy.359
  128.8 1.8 copy.366
  132.5 1.8 reshape.632
  134.3 1.8 copy.374
  149.8 5.2 %collective-permute-start.8 = (bf16[1,1,128,512]{3,2,1,0:T(8,128)(2,1)}, bf16[1,1,128,512]{3,2,1,0:T(8,128)(2,1)}, u32[]{:S(2)}, u32[]{:S(2)}) collective-permute-start(bf16[1,1,128,512]{3,2,1,0:T(8,128)(2,1)} %get-tuple-element.139), channel_id=1, source_target_pairs={{0,4},{4,8},{8,12},{1,5},{5,9},{9,13},{2,6},{6,10},{10,14},{3,7},{... | collective-permute-start | bytes 393224 | tf_op jit(solution)/shard_map/ppermute | solution.py:39
  155.0 7.2 %all-gather.4 = bf16[1,512,512]{2,1,0:T(8,128)(2,1)} all-gather(bf16[1,128,512]{2,1,0:T(8,128)(2,1)} %get-tuple-element.116), channel_id=6, replica_groups=mesh['groups'=2,'rows'=4,'shard'=4] {'shard'}, dimensions={1}, use_global_device_ids=true | all-gather | bytes 655360 | tf_op jit(solution)/shard_map/all_gather | solution.py:122
  162.2 2.6 squeeze.109
  164.8 2.6 squeeze.111
  167.4 2.6 squeeze.112
  170.0 2.6 squeeze.113
  172.6 2.6 squeeze.114
  175.2 2.6 squeeze.115
  177.8 2.8 squeeze.116
  211.7 2.0 pad_slice_fusion.9
  216.1 2.0 reshape.650
  218.0 2.0 reshape.651
  220.0 1.9 reshape.652
  222.0 2.0 reshape.653
  223.9 2.0 reshape.654
  225.9 2.0 reshape.655
  241.4 5.2 %collective-permute-start.10 = (bf16[1,1,128,512]{3,2,1,0:T(8,128)(2,1)}, bf16[1,1,128,512]{3,2,1,0:T(8,128)(2,1)}, u32[]{:S(2)}, u32[]{:S(2)}) collective-permute-start(bf16[1,1,128,512]{3,2,1,0:T(8,128)(2,1)} %copy.489), channel_id=1, source_target_pairs={{0,4},{4,8},{8,12},{1,5},{5,9},{9,13},{2,6},{6,10},{10,14},{3,7},{... | collective-permute-start | bytes 393224 | tf_op jit(solution)/shard_map/ppermute | solution.py:39
  248.5 1.8 gather_fusion.9
  253.1 1.8 gather_fusion.10
  257.0 1.8 gather_fusion.11
  261.0 1.8 gather_fusion.12
  265.0 1.8 gather_fusion.13
  269.0 1.8 gather_fusion.14
  272.9 1.8 gather_fusion.15
  302.3 2.0 reshape.662
  304.3 2.0 reshape.663
  306.3 2.0 reshape.664
  308.2 2.0 reshape.665
  310.2 2.0 reshape.666
  327.0 5.4 %collective-permute-start.12 = (bf16[1,1,128,512]{3,2,1,0:T(8,128)(2,1)}, bf16[1,1,128,512]{3,2,1,0:T(8,128)(2,1)}, u32[]{:S(2)}, u32[]{:S(2)}) collective-permute-start(bf16[1,1,128,512]{3,2,1,0:T(8,128)(2,1)} %copy.493), channel_id=1, source_target_pairs={{0,4},{4,8},{8,12},{1,5},{5,9},{9,13},{2,6},{6,10},{10,14},{3,7},{... | collective-permute-start | bytes 393224 | tf_op jit(solution)/shard_map/ppermute | solution.py:39
  346.1 1.9 gather_fusion.3
  351.7 2.1 convolution_convert_fusion.2
  362.1 1.8 gather_fusion.4
  374.0 1.8 gather_fusion.7
  378.0 1.8 gather_fusion.8
  384.6 8.9 %fusion.61 = (bf16[40,512]{1,0:T(8,128)(2,1)S(1)}, bf16[40,512]{1,0:T(8,128)(2,1)S(1)}) fusion(bf16[144,512]{1,0:T(8,128)(2,1)} %bitcast.77, bf16[144,512]{1,0:T(8,128)(2,1)S(1)} %bitcast.594), kind=kCustom, calls=%all-reduce-scatter.2 | all-reduce-scatter fusion | flops 163841 | bytes 377344
  394.9 4.3 collective-permute-start.14
  405.4 21.7 %reduce-scatter.17.cloned.1.call-done = bf16[128,512]{1,0:T(8,128)(2,1)} async-done(((bf16[512,512]{1,0:T(8,128)(2,1)}), bf16[128,512]{1,0:T(8,128)(2,1)}) %reduce-scatter.17.cloned.1.call-update) | async-done | bytes 131088
  428.9 6.8 %all-gather.5 = bf16[1,512,512]{2,1,0:T(8,128)(2,1)S(1)} all-gather(bf16[1,128,512]{2,1,0:T(8,128)(2,1)S(1)} %copy-done.100), channel_id=7, replica_groups=mesh['groups'=2,'rows'=4,'shard'=4] {'shard'}, dimensions={1}, use_global_device_ids=true | all-gather | bytes 655360 | tf_op jit(solution)/shard_map/all_gather | solution.py:122
  437.7 32.6 %all-reduce.12.cloned.1.call-done = (bf16[2,128,512]{1,2,0:T(8,128)(2,1)}, bf16[2,36,512]{2,1,0:T(8,128)(2,1)}, bf16[2,128,512]{1,2,0:T(8,128)(2,1)}) async-done(((bf16[2,128,512]{1,2,0:T(8,128)(2,1)}, bf16[2,36,512]{2,1,0:T(8,128)(2,1)}, bf16[2,128,512]{1,2,0:T(8,128)(2,1)}), (bf16[2,128,512]{1,2,0:T(8,128)(2,1)}, bf16[2,36,512]{2,1,0:T(8,128)(2,1)}, ...) | async-done | bytes 598032 | tf_op jit(solution)/shard_map/psum | solution.py:188
  (553 shorter events, 215.7 us)
Async XLA Ops:
  7.2 394.3 %reduce-scatter.23.cloned.1.call-start = ((), (), s32[]{:S(2)}) async-start(), calls=%async_computation.7 | async-start | bytes 655360
  9.0 84.1 %collective-permute-start.5 = (bf16[128,512]{1,0:T(8,128)(2,1)}, bf16[128,512]{1,0:T(8,128)(2,1)}, u32[]{:S(2)}, u32[]{:S(2)}) collective-permute-start(bf16[128,512]{1,0:T(8,128)(2,1)} %get-tuple-element.115), channel_id=1, source_target_pairs={{0,1},{1,2},{2,3},{3,0},{4,5},{5,6},{6,7},{7,4},{8,9},{9,10},{10,1... | collective-permute-start | bytes 393224 | tf_op jit(solution)/shard_map/ppermute | solution.py:19
  9.4 98.5 %collective-permute-start.6 = (bf16[128,512]{1,0:T(8,128)(2,1)}, bf16[128,512]{1,0:T(8,128)(2,1)}, u32[]{:S(2)}, u32[]{:S(2)}) collective-permute-start(bf16[128,512]{1,0:T(8,128)(2,1)} %get-tuple-element.115), channel_id=1, source_target_pairs={{0,3},{1,0},{2,1},{3,2},{4,7},{5,4},{6,5},{7,6},{8,11},{9,8},{10,9... | collective-permute-start | bytes 393224 | tf_op jit(solution)/shard_map/ppermute | solution.py:24
  11.4 82.0 %collective-permute-start = (bf16[128,512]{1,0:T(8,128)(2,1)}, bf16[128,512]{1,0:T(8,128)(2,1)}, u32[]{:S(2)}, u32[]{:S(2)}) collective-permute-start(bf16[128,512]{1,0:T(8,128)(2,1)} %get-tuple-element.114), channel_id=1, source_target_pairs={{0,1},{1,2},{2,3},{3,0},{4,5},{5,6},{6,7},{7,4},{8,9},{9,10},{10,1... | collective-permute-start | bytes 393224 | tf_op jit(solution)/shard_map/ppermute | solution.py:19
  12.0 84.2 %collective-permute-start.1 = (bf16[128,512]{1,0:T(8,128)(2,1)}, bf16[128,512]{1,0:T(8,128)(2,1)}, u32[]{:S(2)}, u32[]{:S(2)}) collective-permute-start(bf16[128,512]{1,0:T(8,128)(2,1)} %get-tuple-element.114), channel_id=1, source_target_pairs={{0,3},{1,0},{2,1},{3,2},{4,7},{5,4},{6,5},{7,6},{8,11},{9,8},{10,9... | collective-permute-start | bytes 393224 | tf_op jit(solution)/shard_map/ppermute | solution.py:24
  48.3 2.1 copy-start.65
  67.6 5.3 %copy-start.107 = (bf16[2,128,512]{2,1,0:T(8,128)(2,1)S(1)}, bf16[2,128,512]{2,1,0:T(8,128)(2,1)}, u32[]{:S(2)}) copy-start(bf16[2,128,512]{2,1,0:T(8,128)(2,1)} %param.17) | copy-start | bytes 786436
  70.2 10.8 %copy-start.70 = (bf16[1,2,128,512]{3,2,1,0:T(8,128)(2,1)S(1)}, bf16[1,2,128,512]{3,2,1,0:T(8,128)(2,1)}, u32[]{:S(2)}) copy-start(bf16[1,2,128,512]{3,2,1,0:T(8,128)(2,1)} %param.13) | copy-start | bytes 786436
  93.1 16.5 %collective-permute-start.7 = (bf16[128,512]{1,0:T(8,128)(2,1)}, bf16[128,512]{1,0:T(8,128)(2,1)}, u32[]{:S(2)}, u32[]{:S(2)}) collective-permute-start(bf16[128,512]{1,0:T(8,128)(2,1)} %collective-permute-done.5), channel_id=1, source_target_pairs={{0,1},{1,2},{2,3},{3,0},{4,5},{5,6},{6,7},{7,4},{8,9},{9,10},{10,1... | collective-permute-start | bytes 393224 | tf_op jit(solution)/shard_map/ppermute | solution.py:19
  93.4 5.7 %collective-permute-start.2 = (bf16[128,512]{1,0:T(8,128)(2,1)}, bf16[128,512]{1,0:T(8,128)(2,1)S(1)}, u32[]{:S(2)}, u32[]{:S(2)}) collective-permute-start(bf16[128,512]{1,0:T(8,128)(2,1)} %collective-permute-done), channel_id=1, source_target_pairs={{0,1},{1,2},{2,3},{3,0},{4,5},{5,6},{6,7},{7,4},{8,9},{9,10},{10,1... | collective-permute-start | bytes 393224 | tf_op jit(solution)/shard_map/ppermute | solution.py:19
  94.5 4.6 copy-start.93
  101.9 39.8 %copy-start.2 = (bf16[256,512]{0,1:T(8,128)(2,1)}, bf16[256,512]{0,1:T(8,128)(2,1)S(1)}, u32[]{:S(2)}) copy-start(bf16[256,512]{0,1:T(8,128)(2,1)S(1)} %get-tuple-element.149) | copy-start | bytes 786436
  102.1 9.0 %collective-permute-start.4 = (bf16[1,1,128,512]{3,2,1,0:T(8,128)(2,1)S(1)}, bf16[1,1,128,512]{3,2,1,0:T(8,128)(2,1)S(1)}, u32[]{:S(2)}, u32[]{:S(2)}) collective-permute-start(bf16[1,1,128,512]{3,2,1,0:T(8,128)(2,1)S(1)} %get-tuple-element.144), channel_id=1, source_target_pairs={{4,0},{8,4},{12,8},{5,1},{9,5},{13,9},{6,2},{10,6},{14,10},{7,3},{... | collective-permute-start | bytes 393224 | tf_op jit(solution)/shard_map/ppermute | solution.py:41
  103.4 7.7 %collective-permute-start.3 = (bf16[1,1,128,512]{3,2,1,0:T(8,128)(2,1)S(1)}, bf16[1,1,128,512]{3,2,1,0:T(8,128)(2,1)S(1)}, u32[]{:S(2)}, u32[]{:S(2)}) collective-permute-start(bf16[1,1,128,512]{3,2,1,0:T(8,128)(2,1)S(1)} %get-tuple-element.143), channel_id=1, source_target_pairs={{0,4},{4,8},{8,12},{1,5},{5,9},{9,13},{2,6},{6,10},{10,14},{3,7},{... | collective-permute-start | bytes 393224 | tf_op jit(solution)/shard_map/ppermute | solution.py:39
  117.4 3.6 copy-start.69
  123.5 7.1 %copy-start.68 = (bf16[1,2,128,512]{3,2,1,0:T(8,128)(2,1)S(1)}, bf16[1,2,128,512]{3,2,1,0:T(8,128)(2,1)}, u32[]{:S(2)}) copy-start(bf16[1,2,128,512]{3,2,1,0:T(8,128)(2,1)} %get-tuple-element.104) | copy-start | bytes 786436
  132.5 10.2 %copy-start.4 = (bf16[256,4,128]{0,2,1:T(8,128)(2,1)}, bf16[256,4,128]{0,2,1:T(8,128)(2,1)S(1)}, u32[]{:S(2)}) copy-start(bf16[256,4,128]{0,2,1:T(8,128)(2,1)S(1)} %copy.370) | copy-start | bytes 786436
  145.3 2.4 copy-start
  148.5 35.7 %collective-permute-start.9 = (bf16[1,1,128,512]{3,2,1,0:T(8,128)(2,1)}, bf16[1,1,128,512]{3,2,1,0:T(8,128)(2,1)}, u32[]{:S(2)}, u32[]{:S(2)}) collective-permute-start(bf16[1,1,128,512]{3,2,1,0:T(8,128)(2,1)} %get-tuple-element.140), channel_id=1, source_target_pairs={{4,0},{8,4},{12,8},{5,1},{9,5},{13,9},{6,2},{10,6},{14,10},{7,3},{... | collective-permute-start | bytes 393224 | tf_op jit(solution)/shard_map/ppermute | solution.py:41
  149.8 34.5 %collective-permute-start.8 = (bf16[1,1,128,512]{3,2,1,0:T(8,128)(2,1)}, bf16[1,1,128,512]{3,2,1,0:T(8,128)(2,1)}, u32[]{:S(2)}, u32[]{:S(2)}) collective-permute-start(bf16[1,1,128,512]{3,2,1,0:T(8,128)(2,1)} %get-tuple-element.139), channel_id=1, source_target_pairs={{0,4},{4,8},{8,12},{1,5},{5,9},{9,13},{2,6},{6,10},{10,14},{3,7},{... | collective-permute-start | bytes 393224 | tf_op jit(solution)/shard_map/ppermute | solution.py:39
  189.3 3.2 copy-start.66
  189.6 4.8 copy-start.32
  192.4 2.1 copy-start.63
  199.2 2.0 copy-start.97
  207.8 2.6 copy-start.98
  207.8 2.6 copy-start.106
  207.8 2.6 copy-start.114
  238.8 7.8 %copy-start.86 = (bf16[4,128,128]{2,1,0:T(8,128)(2,1)S(1)}, bf16[4,128,128]{2,1,0:T(8,128)(2,1)}, u32[]{:S(2)}) copy-start(bf16[4,128,128]{2,1,0:T(8,128)(2,1)} %fusion.84) | copy-start | bytes 393220
  239.3 50.6 %collective-permute-start.11 = (bf16[1,1,128,512]{3,2,1,0:T(8,128)(2,1)S(1)}, bf16[1,1,128,512]{3,2,1,0:T(8,128)(2,1)}, u32[]{:S(2)}, u32[]{:S(2)}) collective-permute-start(bf16[1,1,128,512]{3,2,1,0:T(8,128)(2,1)S(1)} %copy.490), channel_id=1, source_target_pairs={{4,0},{8,4},{12,8},{5,1},{9,5},{13,9},{6,2},{10,6},{14,10},{7,3},{... | collective-permute-start | bytes 393224 | tf_op jit(solution)/shard_map/ppermute | solution.py:41
  241.4 48.5 %collective-permute-start.10 = (bf16[1,1,128,512]{3,2,1,0:T(8,128)(2,1)}, bf16[1,1,128,512]{3,2,1,0:T(8,128)(2,1)}, u32[]{:S(2)}, u32[]{:S(2)}) collective-permute-start(bf16[1,1,128,512]{3,2,1,0:T(8,128)(2,1)} %copy.489), channel_id=1, source_target_pairs={{0,4},{4,8},{8,12},{1,5},{5,9},{9,13},{2,6},{6,10},{10,14},{3,7},{... | collective-permute-start | bytes 393224 | tf_op jit(solution)/shard_map/ppermute | solution.py:39
  247.3 3.9 copy-start.84
  251.9 3.3 copy-start.83
  255.8 3.3 copy-start.82
  259.8 3.3 copy-start.81
  263.8 3.3 copy-start.80
  267.7 3.3 copy-start.79
  271.7 3.3 copy-start.78
  275.7 3.3 copy-start.77
  283.0 119.5 %reduce-scatter.19.cloned.1.call-start = ((), (), s32[]{:S(2)}) async-start(), calls=%async_computation.5 | async-start | bytes 655360
  322.7 9.7 %copy-start.88 = (bf16[4,128,128]{2,1,0:T(8,128)(2,1)S(1)}, bf16[4,128,128]{2,1,0:T(8,128)(2,1)}, u32[]{:S(2)}) copy-start(bf16[4,128,128]{2,1,0:T(8,128)(2,1)} %fusion.75) | copy-start | bytes 393220
  324.9 55.3 %collective-permute-start.13 = (bf16[1,1,128,512]{3,2,1,0:T(8,128)(2,1)}, bf16[1,1,128,512]{3,2,1,0:T(8,128)(2,1)}, u32[]{:S(2)}, u32[]{:S(2)}) collective-permute-start(bf16[1,1,128,512]{3,2,1,0:T(8,128)(2,1)} %copy.494), channel_id=1, source_target_pairs={{4,0},{8,4},{12,8},{5,1},{9,5},{13,9},{6,2},{10,6},{14,10},{7,3},{... | collective-permute-start | bytes 393224 | tf_op jit(solution)/shard_map/ppermute | solution.py:41
  327.0 53.3 %collective-permute-start.12 = (bf16[1,1,128,512]{3,2,1,0:T(8,128)(2,1)}, bf16[1,1,128,512]{3,2,1,0:T(8,128)(2,1)}, u32[]{:S(2)}, u32[]{:S(2)}) collective-permute-start(bf16[1,1,128,512]{3,2,1,0:T(8,128)(2,1)} %copy.493), channel_id=1, source_target_pairs={{0,4},{4,8},{8,12},{1,5},{5,9},{9,13},{2,6},{6,10},{10,14},{3,7},{... | collective-permute-start | bytes 393224 | tf_op jit(solution)/shard_map/ppermute | solution.py:39
  333.0 3.3 copy-start.87
  337.0 3.3 copy-start.85
  341.0 3.3 copy-start.89
  346.1 4.4 copy-start.3
  346.1 5.3 %copy-start.11 = (bf16[256,4,128]{0,2,1:T(8,128)(2,1)S(1)}, bf16[256,4,128]{0,2,1:T(8,128)(2,1)}, u32[]{:S(2)}) copy-start(bf16[256,4,128]{0,2,1:T(8,128)(2,1)} %copy.366) | copy-start | bytes 786436
  348.1 3.5 copy-start.76
  351.6 3.4 copy-start.5
  353.8 2.2 copy-start.7
  353.8 2.4 copy-start.9
  353.8 2.7 copy-start.1
  353.8 49.8 %reduce-scatter.21.cloned.1.call-start = ((), (), s32[]{:S(2)}) async-start(), calls=%async_computation.6 | async-start | bytes 655360
  364.9 3.3 copy-start.90
  378.0 2.2 copy-start.109
  380.1 47.0 %reduce-scatter.17.cloned.1.call-start = ((), (), s32[]{:S(2)}) async-start(), calls=%async_computation.4 | async-start | bytes 655360
  383.5 15.7 %copy-start.112 = (u32[32]{0:T(128)S(1)}, u32[32]{0:T(128)}, u32[]{:S(2)}) copy-start(u32[32]{0:T(128)} %constant.436) | copy-start | bytes 388
  384.5 85.8 %all-reduce.12.cloned.1.call-start = ((), (), s32[]{:S(2)}) async-start(), calls=%async_computation.8 | async-start | bytes 1212416 | tf_op jit(solution)/shard_map/psum | solution.py:188
  393.5 6.9 %collective-permute-start.15 = (bf16[12,512]{1,0:T(8,128)(2,1)S(1)}, bf16[12,512]{1,0:T(8,128)(2,1)S(1)}, u32[]{:S(2)}, u32[]{:S(2)}) collective-permute-start(bf16[12,512]{1,0:T(8,128)(2,1)S(1)} %slice.573), channel_id=1, source_target_pairs={{0,1},{1,2},{2,3},{4,5},{5,6},{6,7},{8,9},{9,10},{10,11},{12,13},{... | collective-permute-start | bytes 36872
  394.9 5.7 %collective-permute-start.14 = (bf16[12,512]{1,0:T(8,128)(2,1)S(1)}, bf16[12,512]{1,0:T(8,128)(2,1)S(1)}, u32[]{:S(2)}, u32[]{:S(2)}) collective-permute-start(bf16[12,512]{1,0:T(8,128)(2,1)S(1)} %slice.572), channel_id=1, source_target_pairs={{0,1},{1,2},{2,3},{4,5},{5,6},{6,7},{8,9},{9,10},{10,11},{12,13},{... | collective-permute-start | bytes 36872
  403.6 25.4 %copy-start.100 = (bf16[1,128,512]{2,1,0:T(8,128)(2,1)S(1)}, bf16[1,128,512]{2,1,0:T(8,128)(2,1)}, u32[]{:S(2)}) copy-start(bf16[1,128,512]{2,1,0:T(8,128)(2,1)} %get-tuple-element.113) | copy-start | bytes 393220
  405.4 30.3 %copy-start.108 = (bf16[256,512]{0,1:T(8,128)(2,1)S(1)}, bf16[256,512]{0,1:T(8,128)(2,1)}, u32[]{:S(2)}) copy-start(bf16[256,512]{0,1:T(8,128)(2,1)} %get-tuple-element.153) | copy-start | bytes 786436
  470.3 2.0 copy-start.110
  470.3 2.8 copy-start.104
  (72 other events, 82.5 us)
Sparse Core Ops, SparseCore 0:
  283.1 21.9 reduce-scatter.22
  353.9 21.9 reduce-scatter.18
  380.3 21.9 reduce-scatter.20
  405.3 21.7 reduce-scatter.16
  430.1 40.1 all-reduce.11
